TPU v7x, 512 devices: a whole 4x4x16 slice. The times are simulated.
512 devices in a mesh: shape: 16 (over z_lo, x), query: 32 (over z_hi, y, core).
Axes of the slice: x: 4, y: 4, z: 16 (z_hi: 4, z_lo: 4; z = z_hi * 4 + z_lo), core: 2. Of those that a mesh axis runs over, the one named last changes fastest.
Arguments:
- queries: bfloat16 [16, 4096, 512], P('shape', 'query'), may hold values from -128 to 128
- keys: bfloat16 [16, 1024, 512], P('shape', 'query'), may hold values from -5 to 5
- values: bfloat16 [16, 1024, 512], P('shape', 'query'), may hold values from -6 to 6
- out_weight: bfloat16 [512, 512], replicated, may hold values from -0.25 to 0.25
- out_grad: float32 [16, 4096, 512], P('shape', 'query'), may hold values from -6 to 6
Outputs:
- query_grad: float32 [16, 4096, 512], P('shape', 'query')
- key_grad: float32 [16, 1024, 512], P('shape', 'query')
- value_grad: float32 [16, 1024, 512], P('shape', 'query')
- weight_grad: float32 [512, 512], replicated
All inputs are finite; a program needn't handle non-finite values.
Results may differ from a plain program's by a relative error of at most 0.02.
Values may be sent and summed in bfloat16 or wider, within the bound.
A program may use at most 64 MiB of HBM per device.

v0:
```python
import math
import jax
import jax.numpy as jnp
from jax import lax
from jax.sharding import PartitionSpec as P

HEADS = 8
HEAD = 64


def shards(queries, keys, values, out_weight, out_grad):
    lat_rows = keys.shape[1]
    width = queries.shape[2]
    scale = 1.0 / math.sqrt(HEAD)
    shape_count = lax.axis_size("shape")
    members = lax.axis_size("query")
    query_rows = queries[0]
    grad_b = out_grad[0].astype(jnp.bfloat16)
    d_attn = jnp.einsum("tf,df->td", grad_b, out_weight, preferred_element_type=jnp.float32).astype(
        jnp.bfloat16
    )
    key_all, value_all = (
        lax.all_gather(keys[0], "query", axis=0, tiled=True),
        lax.all_gather(values[0], "query", axis=0, tiled=True),
    )
    grad_list, attn_list, key_list, value_list = ([], [], [], [])
    for head_index in range(HEADS):
        cols = slice(head_index * HEAD, (head_index + 1) * HEAD)
        q_head = query_rows[:, cols]
        key_head = key_all[:, cols]
        value_head = value_all[:, cols]
        scores = jnp.dot(q_head, key_head.T, preferred_element_type=jnp.float32) * scale
        top = jnp.max(scores, axis=1, keepdims=True)
        lse = top + jnp.log(jnp.sum(jnp.exp(scores - top), axis=1, keepdims=True))
        probs = jnp.exp(scores - lse)
        probs_b = probs.astype(jnp.bfloat16)
        attn_b = jnp.dot(probs_b, value_head, preferred_element_type=jnp.float32).astype(
            jnp.bfloat16
        )
        d_head = d_attn[:, cols]
        delta = jnp.sum(
            d_head.astype(jnp.float32) * attn_b.astype(jnp.float32), axis=1, keepdims=True
        )
        d_probs = jnp.dot(d_head, value_head.T, preferred_element_type=jnp.float32)
        d_scores = (probs * (d_probs - delta) * scale).astype(jnp.bfloat16)
        grad_list.append(jnp.dot(d_scores, key_head, preferred_element_type=jnp.float32))
        key_list.append(
            jnp.einsum("tm,td->md", d_scores, q_head, preferred_element_type=jnp.float32)
        )
        value_list.append(
            jnp.einsum("tm,td->md", probs_b, d_head, preferred_element_type=jnp.float32)
        )
        attn_list.append(attn_b)
    query_grad = jnp.concatenate(grad_list, axis=1)
    attn = jnp.concatenate(attn_list, axis=1)
    key_terms = jnp.concatenate(key_list, axis=1).reshape(members, lat_rows, width)
    value_terms = jnp.concatenate(value_list, axis=1).reshape(members, lat_rows, width)
    key_in, value_in = (
        lax.all_to_all(key_terms, "query", split_axis=0, concat_axis=0, tiled=True),
        lax.all_to_all(value_terms, "query", split_axis=0, concat_axis=0, tiled=True),
    )
    key_grad = jnp.sum(key_in, axis=0)
    value_grad = jnp.sum(value_in, axis=0)
    weight_term = jnp.einsum("td,tf->df", attn, grad_b, preferred_element_type=jnp.float32) * (
        1.0 / shape_count
    )
    weight_grad = lax.psum(weight_term, ("shape", "query"))
    return (query_grad[None], key_grad[None], value_grad[None], weight_grad)


def solution(mesh):
    return jax.shard_map(
        shards,
        mesh=mesh,
        in_specs=(
            P("shape", "query", None),
            P("shape", "query", None),
            P("shape", "query", None),
            P(),
            P("shape", "query", None),
        ),
        out_specs=(
            P("shape", "query", None),
            P("shape", "query", None),
            P("shape", "query", None),
            P(),
        ),
        check_vma=False,
    )
```

profile of v0, /device:TPU:1, one launch (start us, length us, event | category | flops | bytes accessed | tf_op | source)
XLA Modules:
  0.0 804.2 jit_solution(14749125188669435958)
XLA Ops:
  7.2 0.7 all-gather.5.cloned.1.call-update
  7.9 0.3 copy-done
  8.2 1.3 convolution_convert_fusion
  9.5 79.2 %all-gather.5.cloned.1.call-done = bf16[1,1024,512]{2,1,0:T(8,128)(2,1)} async-done(((bf16[1,32,512]{2,1,0:T(8,128)(2,1)}), bf16[1,1024,512]{2,1,0:T(8,128)(2,1)}) %all-gather.5.cloned.1.call-update) | async-done | bytes 1048592 | tf_op jit(solution)/shard_map/all_gather | solution.py:23
  88.7 1.4 fusion.117
  90.1 1.6 fusion.118
  91.6 1.5 fusion.119
  93.1 0.4 fusion.120
  93.5 0.3 fusion.121
  93.8 0.4 fusion.122
  94.2 0.3 fusion.123
  94.6 0.4 fusion.116
  97.0 1.0 convolution_dynamic-update-slice_fusion.7
  98.0 1.0 convolution_dynamic-update-slice_fusion.6
  99.0 1.0 convolution_dynamic-update-slice_fusion.5
  100.0 1.0 convolution_dynamic-update-slice_fusion.4
  101.0 1.0 convolution_dynamic-update-slice_fusion.3
  102.0 1.0 convolution_dynamic-update-slice_fusion.2
  103.0 1.0 convolution_dynamic-update-slice_fusion.1
  104.0 1.0 convolution_dynamic-update-slice_fusion
  105.0 2.9 copy.27
  107.9 7.5 all-to-all-start.1
  115.4 0.7 all-gather.7.cloned.1.call-update
  116.1 140.1 %all-gather.7.cloned.1.call-done = bf16[1,1024,512]{2,1,0:T(8,128)(2,1)} async-done(((bf16[1,32,512]{2,1,0:T(8,128)(2,1)}), bf16[1,1024,512]{2,1,0:T(8,128)(2,1)}) %all-gather.7.cloned.1.call-update) | async-done | bytes 1048592 | tf_op jit(solution)/shard_map/all_gather | solution.py:24
  256.3 1.4 convolution_convert_fusion.2
  257.7 1.3 convolution_convert_fusion.3
  259.1 1.3 convolution_convert_fusion.4
  260.4 0.3 convolution_convert_fusion.5
  260.8 0.3 convolution_convert_fusion.6
  261.1 0.3 convolution_convert_fusion.7
  261.5 0.3 convolution_convert_fusion.8
  261.8 1.0 multiply_reduce_fusion
  262.8 0.9 fusion.23
  263.7 0.9 convolution_dynamic-update-slice_fusion.15
  264.7 0.3 fusion.22
  265.0 1.0 convolution_dynamic-update-slice_fusion.14
  266.0 0.3 fusion.21
  266.3 0.9 convolution_dynamic-update-slice_fusion.13
  267.2 0.3 fusion.20
  267.5 1.0 convolution_dynamic-update-slice_fusion.12
  268.6 0.3 fusion.19
  268.8 0.9 convolution_dynamic-update-slice_fusion.11
  269.8 0.3 fusion.18
  270.1 1.0 convolution_dynamic-update-slice_fusion.10
  271.1 0.3 fusion.17
  271.4 0.9 convolution_dynamic-update-slice_fusion.9
  272.3 0.3 fusion.16
  272.6 1.0 convolution_dynamic-update-slice_fusion.8
  273.6 2.9 copy.26
  276.7 7.6 all-to-all-start
  284.8 2.3 convolution_multiply_fusion
  287.1 0.2 convolution_dynamic-update-slice_fusion.23
  287.4 0.4 convolution_dynamic-update-slice_fusion.22
  288.0 0.4 convolution_dynamic-update-slice_fusion.20
  288.4 0.2 convolution_dynamic-update-slice_fusion.19
  288.7 0.4 convolution_dynamic-update-slice_fusion.18
  289.3 0.4 convolution_dynamic-update-slice_fusion.16
  289.7 0.7 copy-done.25
  290.4 1.8 copy.28
  292.2 2.4 reduce_sum.179
  294.5 90.0 %all-to-all-done = f32[32,32,512]{2,1,0:T(8,128)} async-done(((f32[32,32,512]{2,1,0:T(8,128)}), f32[32,32,512]{2,1,0:T(8,128)}, u32[]{:S(2)}, u32[]{:S(2)}) %all-to-all-start) | async-done | bytes 2097184 | tf_op jit(solution)/shard_map/all_to_all | solution.py:59
  384.6 2.4 reduce_sum.178
  386.9 408.5 %all-reduce.2.cloned.1.call-done = f32[512,512]{1,0:T(8,128)} async-done(((f32[512,512]{1,0:T(8,128)}), f32[512,512]{1,0:T(8,128)}) %all-reduce.2.cloned.1.call-update) | async-done | bytes 1048592 | tf_op jit(solution)/shard_map/psum | solution.py:67
  795.4 2.3 copy.59
  (118 shorter events, 3.0 us)
Async XLA Ops:
  7.2 1.0 copy-start
  7.2 84.4 %copy-start.23 = (bf16[1,128,512]{2,1,0:T(8,128)(2,1)S(1)}, bf16[1,128,512]{2,1,0:T(8,128)(2,1)}, u32[]{:S(2)}) copy-start(bf16[1,128,512]{2,1,0:T(8,128)(2,1)} %param.5) | copy-start | bytes 393220
  7.2 81.5 %all-gather.5.cloned.1.call-start = ((), (), s32[]{:S(2)}) async-start(), calls=%async_computation.3 | async-start | bytes 1081344 | tf_op jit(solution)/shard_map/all_gather | solution.py:23
  88.7 4.4 copy-start.1
  90.0 6.9 copy-start.9
  91.6 6.4 copy-start.7
  93.1 5.9 copy-start.5
  93.5 6.5 copy-start.3
  95.0 9.0 %copy-start.11 = (f32[128,1024]{1,0:T(8,128)}, f32[128,1024]{1,0:T(8,128)S(1)}, u32[]{:S(2)}) copy-start(f32[128,1024]{1,0:T(8,128)S(1)} %get-tuple-element.21) | copy-start | bytes 1572868
  95.2 166.2 %copy-start.43 = (f32[128]{0:T(128)}, f32[128]{0:T(128)S(1)}, u32[]{:S(2)}) copy-start(f32[128]{0:T(128)S(1)} %log_add_fusion.7) | copy-start | bytes 1540
  95.5 165.6 %copy-start.44 = (f32[128]{0:T(128)}, f32[128]{0:T(128)S(1)}, u32[]{:S(2)}) copy-start(f32[128]{0:T(128)S(1)} %log_add_fusion.6) | copy-start | bytes 1540
  95.7 165.0 %copy-start.41 = (f32[128]{0:T(128)}, f32[128]{0:T(128)S(1)}, u32[]{:S(2)}) copy-start(f32[128]{0:T(128)S(1)} %log_add_fusion.5) | copy-start | bytes 1540
  97.0 164.8 %copy-start.46 = (f32[128]{0:T(128)}, f32[128]{0:T(128)S(1)}, u32[]{:S(2)}) copy-start(f32[128]{0:T(128)S(1)} %log_add_fusion) | copy-start | bytes 1540
  107.9 168.7 %all-to-all-start.1 = ((f32[32,32,512]{2,1,0:T(8,128)}), f32[32,32,512]{2,1,0:T(8,128)}, u32[]{:S(2)}, u32[]{:S(2)}) async-start(f32[32,32,512]{2,1,0:T(8,128)} %bitcast.63), calls=%async_computation.1 | async-start | bytes 4194304 | tf_op jit(solution)/shard_map/all_to_all | solution.py:60
  115.4 140.9 %all-gather.7.cloned.1.call-start = ((), (), s32[]{:S(2)}) async-start(), calls=%async_computation.4 | async-start | bytes 1081344 | tf_op jit(solution)/shard_map/all_gather | solution.py:24
  256.3 4.1 copy-start.2
  256.3 4.1 copy-start.4
  256.3 4.5 copy-start.6
  256.3 4.8 copy-start.8
  257.7 4.1 copy-start.26
  257.7 3.8 copy-start.10
  259.0 3.7 copy-start.28
  259.1 2.7 copy-start.12
  260.4 2.4 copy-start.30
  260.8 2.9 copy-start.32
  261.1 3.6 copy-start.34
  261.1 2.6 copy-start.24
  261.5 3.5 copy-start.36
  261.5 3.2 copy-start.45
  261.8 4.2 copy-start.38
  261.8 4.2 copy-start.42
  265.0 3.8 copy-start.13
  266.3 3.8 copy-start.15
  267.5 3.8 copy-start.17
  268.8 3.8 copy-start.19
  268.8 3.5 copy-start.47
  272.6 4.0 copy-start.21
  276.6 8.0 copy-start.27
  276.6 8.0 copy-start.29
  276.6 8.0 copy-start.31
  276.6 8.0 copy-start.33
  276.6 8.0 copy-start.35
  276.6 8.0 copy-start.37
  276.6 8.0 copy-start.39
  276.6 8.0 copy-start.40
  276.7 107.9 %all-to-all-start = ((f32[32,32,512]{2,1,0:T(8,128)}), f32[32,32,512]{2,1,0:T(8,128)}, u32[]{:S(2)}, u32[]{:S(2)}) async-start(f32[32,32,512]{2,1,0:T(8,128)} %bitcast.64), calls=%async_computation | async-start | bytes 4194304 | tf_op jit(solution)/shard_map/all_to_all | solution.py:59
  284.3 3.1 copy-start.14
  284.3 3.5 copy-start.16
  284.3 511.1 %all-reduce.2.cloned.1.call-start = ((), (), s32[]{:S(2)}) async-start(), calls=%async_computation.2 | async-start | bytes 2097152 | tf_op jit(solution)/shard_map/psum | solution.py:67
  284.8 3.2 copy-start.18
  284.8 3.6 copy-start.20
  287.1 2.2 copy-start.22
  289.7 0.7 copy-start.25
Sparse Core Ops, SparseCore 0:
  11.2 77.4 all-gather.4
  119.4 136.8 all-gather.6
  291.2 504.1 all-reduce.1
where the time goes:
time: 805 us; the launch traced here: 804 us
  waiting for transfers between devices  719 us (89%)
  matrix products  37.1 us (5%)
  starting transfers between devices  15.4 us (2%)
  between operations  14.6 us (2%)
  local copies, waits for them, and re-layouts  11.2 us (1%)
    psum x1, waiting for transfers between devices, shards(): weight_grad = lax.psum(weight_term, ('shape', 'query'))  408 us
    all_gather x1, waiting for transfers between devices, shards(): lax.all_gather(values[0], 'query', axis=0, tiled=True)  140 us
    all_to_all x1, waiting for transfers between devices, shards(): lax.all_to_all(key_terms, 'query', split_axis=0, concat_axis=0, tiled=True)  90 us
    all_gather x1, waiting for transfers between devices, shards(): lax.all_gather(keys[0], 'query', axis=0, tiled=True)  79.2 us
  transfers between devices with their start and end apart: 5, of which 4 were waited for; matrix products, arithmetic and copies ran while one was open for 4% of the time, Pallas kernels for 0%

commit v1 on v0

--- a/solution.py
+++ b/solution.py
@@ -64,7 +64,7 @@
     weight_term = jnp.einsum("td,tf->df", attn, grad_b, preferred_element_type=jnp.float32) * (
         1.0 / shape_count
     )
-    weight_grad = lax.psum(weight_term, ("shape", "query"))
+    weight_grad = lax.psum(lax.psum(weight_term, "shape"), "query")
     return (query_grad[None], key_grad[None], value_grad[None], weight_grad)
 
 

time: 805 us -> 863 us (1.072)
  waiting for transfers between devices: 719 us -> 775 us
    psum x1 -> x2, waiting for transfers between devices: 408 us -> 555 us  [shards(): weight_grad = lax.psum(lax.psum(weight_term, 'shape'), 'query')]
    all_to_all x1, waiting for transfers between devices: 90 us -> 0.01 us  [shards(): lax.all_to_all(key_terms, 'query', split_axis=0, concat_axis=0, tiled=True)]
  transfers between devices with their start and end apart: 5 -> 6, of which waited for: 4 -> 4; matrix products, arithmetic and copies ran while one was open for 4% -> 4% of each run, Pallas kernels for 0% -> 0%
where the time goes in v1:
time: 863 us
  waiting for transfers between devices  775 us (90%)
  matrix products  40.3 us (5%)
  starting transfers between devices  15.3 us (2%)
  between operations  14.5 us (2%)
  local copies, waits for them, and re-layouts  10.5 us (1%)
    psum x2, waiting for transfers between devices, shards(): weight_grad = lax.psum(lax.psum(weight_term, 'shape'), 'query')  555 us
    all_gather x1, waiting for transfers between devices, shards(): lax.all_gather(values[0], 'query', axis=0, tiled=True)  140 us
    all_gather x1, waiting for transfers between devices, shards(): lax.all_gather(keys[0], 'query', axis=0, tiled=True)  79.2 us
  transfers between devices with their start and end apart: 6, of which 4 were waited for; matrix products, arithmetic and copies ran while one was open for 4% of the time, Pallas kernels for 0%

profile of v1, /device:TPU:1, one launch (start us, length us, event | category | flops | bytes accessed | tf_op | source)
XLA Modules:
  0.0 862.7 jit_solution(14418367302656456988)
XLA Ops:
  7.2 0.7 all-gather.5.cloned.1.call-update
  7.9 0.3 copy-done
  8.2 1.3 convolution_convert_fusion
  9.5 79.2 %all-gather.5.cloned.1.call-done = bf16[1,1024,512]{2,1,0:T(8,128)(2,1)} async-done(((bf16[1,32,512]{2,1,0:T(8,128)(2,1)}), bf16[1,1024,512]{2,1,0:T(8,128)(2,1)}) %all-gather.5.cloned.1.call-update) | async-done | bytes 1048592 | tf_op jit(solution)/shard_map/all_gather | solution.py:23
  88.7 1.4 fusion.117
  90.0 1.6 fusion.118
  91.6 1.5 fusion.119
  93.1 0.4 fusion.120
  93.5 0.3 fusion.121
  93.8 0.4 fusion.122
  94.2 0.3 fusion.123
  94.6 0.4 fusion.116
  97.0 1.0 convolution_dynamic-update-slice_fusion.7
  98.0 1.0 convolution_dynamic-update-slice_fusion.6
  99.0 1.0 convolution_dynamic-update-slice_fusion.5
  100.0 1.0 convolution_dynamic-update-slice_fusion.4
  101.0 1.0 convolution_dynamic-update-slice_fusion.3
  102.0 1.0 convolution_dynamic-update-slice_fusion.2
  103.0 1.0 convolution_dynamic-update-slice_fusion.1
  104.0 1.0 convolution_dynamic-update-slice_fusion
  105.0 2.9 copy.27
  107.9 7.5 all-to-all-start.1
  115.4 0.7 all-gather.7.cloned.1.call-update
  116.1 139.8 %all-gather.7.cloned.1.call-done = bf16[1,1024,512]{2,1,0:T(8,128)(2,1)} async-done(((bf16[1,32,512]{2,1,0:T(8,128)(2,1)}), bf16[1,1024,512]{2,1,0:T(8,128)(2,1)}) %all-gather.7.cloned.1.call-update) | async-done | bytes 1048592 | tf_op jit(solution)/shard_map/all_gather | solution.py:24
  255.9 1.4 convolution_convert_fusion.2
  257.3 1.3 convolution_convert_fusion.3
  258.7 1.3 convolution_convert_fusion.4
  260.0 0.3 convolution_convert_fusion.5
  260.4 0.3 convolution_convert_fusion.6
  260.7 0.3 convolution_convert_fusion.7
  261.1 0.3 convolution_convert_fusion.8
  261.4 1.0 multiply_reduce_fusion
  262.7 0.9 convolution_dynamic-update-slice_fusion.15
  263.6 0.3 fusion.22
  263.9 1.0 convolution_dynamic-update-slice_fusion.14
  264.9 0.3 fusion.21
  265.2 0.9 convolution_dynamic-update-slice_fusion.13
  266.2 0.3 fusion.20
  266.5 1.0 convolution_dynamic-update-slice_fusion.12
  267.5 0.3 fusion.19
  267.8 0.9 convolution_dynamic-update-slice_fusion.11
  268.7 0.3 fusion.18
  269.1 1.0 convolution_dynamic-update-slice_fusion.10
  270.0 0.3 fusion.17
  270.3 0.9 convolution_dynamic-update-slice_fusion.9
  271.2 0.3 fusion.16
  271.6 1.0 convolution_dynamic-update-slice_fusion.8
  272.6 2.9 copy.26
  275.6 7.6 all-to-all-start
  283.6 1.3 convolution_multiply_fusion
  285.0 0.8 convolution_dynamic-update-slice_fusion.23
  285.8 1.0 convolution_dynamic-update-slice_fusion.22
  286.8 0.8 convolution_dynamic-update-slice_fusion.21
  287.7 203.1 %all-reduce.3.cloned.1.call-done = f32[512,512]{1,0:T(8,128)} async-done(((f32[512,512]{1,0:T(8,128)}), f32[512,512]{1,0:T(8,128)}) %all-reduce.3.cloned.1.call-update) | async-done | bytes 1048592 | tf_op jit(solution)/shard_map/psum | solution.py:67
  490.8 1.0 convolution_dynamic-update-slice_fusion.20
  491.8 0.9 convolution_dynamic-update-slice_fusion.19
  492.7 1.0 convolution_dynamic-update-slice_fusion.18
  493.6 0.8 convolution_dynamic-update-slice_fusion.17
  494.5 1.0 convolution_dynamic-update-slice_fusion.16
  495.5 1.8 copy.28
  497.3 2.4 reduce_sum.179
  499.6 2.4 reduce_sum.178
  502.0 352.0 %all-reduce.5.cloned.1.call-done = f32[512,512]{1,0:T(8,128)} async-done(((f32[512,512]{1,0:T(8,128)}), f32[512,512]{1,0:T(8,128)}) %all-reduce.5.cloned.1.call-update) | async-done | bytes 1048592 | tf_op jit(solution)/shard_map/psum | solution.py:67
  854.0 2.3 copy.60
  (115 shorter events, 2.7 us)
Async XLA Ops:
  7.2 1.0 copy-start
  7.2 84.4 %copy-start.25 = (bf16[1,128,512]{2,1,0:T(8,128)(2,1)S(1)}, bf16[1,128,512]{2,1,0:T(8,128)(2,1)}, u32[]{:S(2)}) copy-start(bf16[1,128,512]{2,1,0:T(8,128)(2,1)} %param.5) | copy-start | bytes 393220
  7.2 81.5 %all-gather.5.cloned.1.call-start = ((), (), s32[]{:S(2)}) async-start(), calls=%async_computation.4 | async-start | bytes 1081344 | tf_op jit(solution)/shard_map/all_gather | solution.py:23
  88.7 4.4 copy-start.1
  90.0 6.9 copy-start.9
  91.6 6.3 copy-start.7
  93.1 5.9 copy-start.5
  93.5 6.5 copy-start.3
  95.0 9.0 %copy-start.11 = (f32[128,1024]{1,0:T(8,128)}, f32[128,1024]{1,0:T(8,128)S(1)}, u32[]{:S(2)}) copy-start(f32[128,1024]{1,0:T(8,128)S(1)} %get-tuple-element.21) | copy-start | bytes 1572868
  97.0 164.4 %copy-start.43 = (f32[128]{0:T(128)}, f32[128]{0:T(128)S(1)}, u32[]{:S(2)}) copy-start(f32[128]{0:T(128)S(1)} %log_add_fusion) | copy-start | bytes 1540
  107.9 167.7 %all-to-all-start.1 = ((f32[32,32,512]{2,1,0:T(8,128)}), f32[32,32,512]{2,1,0:T(8,128)}, u32[]{:S(2)}, u32[]{:S(2)}) async-start(f32[32,32,512]{2,1,0:T(8,128)} %bitcast.63), calls=%async_computation.1 | async-start | bytes 4194304 | tf_op jit(solution)/shard_map/all_to_all | solution.py:60
  115.4 140.5 %all-gather.7.cloned.1.call-start = ((), (), s32[]{:S(2)}) async-start(), calls=%async_computation.5 | async-start | bytes 1081344 | tf_op jit(solution)/shard_map/all_gather | solution.py:24
  255.9 4.1 copy-start.2
  255.9 4.1 copy-start.4
  255.9 4.5 copy-start.6
  255.9 4.8 copy-start.8
  257.3 4.1 copy-start.28
  257.3 3.7 copy-start.10
  258.7 3.7 copy-start.30
  258.7 2.7 copy-start.12
  260.0 2.3 copy-start.32
  260.4 2.0 copy-start.34
  260.7 1.7 copy-start.36
  261.1 1.3 copy-start.38
  261.4 1.0 copy-start.40
  262.7 3.8 copy-start.13
  263.6 2.9 copy-start.26
  263.9 3.8 copy-start.17
  265.2 3.8 copy-start.21
  267.8 3.8 copy-start.15
  267.8 3.5 copy-start.44
  269.1 2.5 copy-start.19
  271.6 4.0 copy-start.23
  275.5 7.8 copy-start.29
  275.5 7.8 copy-start.31
  275.6 7.8 copy-start.33
  275.6 7.8 copy-start.35
  275.6 7.8 copy-start.37
  275.6 7.8 copy-start.39
  275.6 7.8 copy-start.41
  275.6 7.8 copy-start.42
  275.6 8.0 copy-start.27
  275.6 224.0 %all-to-all-start = ((f32[32,32,512]{2,1,0:T(8,128)}), f32[32,32,512]{2,1,0:T(8,128)}, u32[]{:S(2)}, u32[]{:S(2)}) async-start(f32[32,32,512]{2,1,0:T(8,128)} %bitcast.64), calls=%async_computation | async-start | bytes 4194304 | tf_op jit(solution)/shard_map/all_to_all | solution.py:59
  283.3 1.7 copy-start.14
  283.3 2.5 copy-start.18
  283.3 3.5 copy-start.22
  283.3 207.5 %all-reduce.3.cloned.1.call-start = ((), (), s32[]{:S(2)}) async-start(), calls=%async_computation.2 | async-start | bytes 2097152 | tf_op jit(solution)/shard_map/psum | solution.py:67
  284.9 206.9 %copy-start.16 = (bf16[128,1024]{1,0:T(8,128)(2,1)S(1)}, bf16[128,1024]{1,0:T(8,128)(2,1)}, u32[]{:S(2)}) copy-start(bf16[128,1024]{1,0:T(8,128)(2,1)} %copy-done.15) | copy-start | bytes 786436
  284.9 207.8 %copy-start.20 = (bf16[128,1024]{1,0:T(8,128)(2,1)S(1)}, bf16[128,1024]{1,0:T(8,128)(2,1)}, u32[]{:S(2)}) copy-start(bf16[128,1024]{1,0:T(8,128)(2,1)} %copy-done.19) | copy-start | bytes 786436
  284.9 569.1 %all-reduce.5.cloned.1.call-start = ((), (), s32[]{:S(2)}) async-start(), calls=%async_computation.3 | async-start | bytes 2097152 | tf_op jit(solution)/shard_map/psum | solution.py:67
  285.8 208.7 %copy-start.24 = (bf16[128,1024]{1,0:T(8,128)(2,1)S(1)}, bf16[128,1024]{1,0:T(8,128)(2,1)}, u32[]{:S(2)}) copy-start(bf16[128,1024]{1,0:T(8,128)(2,1)} %copy-done.23) | copy-start | bytes 786436
Sparse Core Ops, SparseCore 0:
  11.2 77.4 all-gather.4
  119.4 136.5 all-gather.6
  287.6 203.1 all-reduce.2
  493.8 360.0 all-reduce.4
